TPU v7x, 128 devices: a whole 4x4x4 slice. The times are simulated.
128 devices in a mesh: section: 4 (over x_lo, core), fsdp: 32 (over x_hi, z, y).
Axes of the slice: x: 4 (x_hi: 2, x_lo: 2; x = x_hi * 2 + x_lo), y: 4, z: 4, core: 2. Of those that a mesh axis runs over, the one named last changes fastest.
Arguments:
- saved_inputs: bfloat16 [4, 2, 32, 512, 1536], P('section', None, 'fsdp'), may hold values from -6 to 6
- grad_outputs: bfloat16 [2, 32, 512, 1536], P(None, 'fsdp'), may hold values from -6 to 6
- lengths: int32 [2, 32], P(None, 'fsdp'), may hold values from 256 to 512, as said below
- pointwise: bfloat16 [4, 1536, 1536], P('section', 'fsdp'), may hold values from -0.15625 to 0.15625
- depth_kernel: bfloat16 [4, 5, 1536], P('section', None, 'fsdp'), may hold values from -2.5 to 2.5
- norm_gain: bfloat16 [4, 1536], P('section', 'fsdp'), may hold values from 0.5 to 1.5
Outputs:
- frame_grads: bfloat16 [4, 2, 32, 512, 1536], P('section', None, 'fsdp')
- pointwise_grad: float32 [4, 1536, 1536], P('section', 'fsdp')
- kernel_grad: float32 [4, 5, 1536], P('section', None, 'fsdp')
- gain_grad: float32 [4, 1536], P('section', 'fsdp')
Inputs may be any that keep to these rules, and one draw needn't show every extreme that they name: `lengths`: frames at and after an utterance's length are padding; some utterance fills all 512 slots.
All inputs are finite; a program needn't handle non-finite values.
Results may differ from a plain program's by a relative error of at most 0.0057.
Values may be sent and summed in bfloat16 or wider, within the bound.
No kernel may reach another device: no remote copies, remote signals or barrier semaphores. Data moves between devices by JAX's collectives and lax.ppermute only.
A program may use at most 128 MiB of HBM per device.

v0:
```python
import jax
import jax.numpy as jnp
from jax import lax
from jax.sharding import PartitionSpec as P

EPSILON = 1e-05


def shifted(block, axis, distance):
    devices = range(lax.axis_size(axis))
    route = [(i - distance, i) for i in devices if i - distance in devices]
    return lax.ppermute(block, axis, route)


def depthwise(signal, kernel):
    tap_count = kernel.shape[0]
    margin = (tap_count - 1) // 2
    length = signal.shape[-2]
    widths = [(0, 0)] * (signal.ndim - 2) + [(margin, margin), (0, 0)]
    padded = jnp.pad(signal, widths)
    running = jnp.zeros(signal.shape, jnp.float32)
    for offset in range(tap_count):
        running = (
            running + kernel[offset].astype(jnp.float32) * padded[..., offset : offset + length, :]
        )
    return running


def tap_sums(upstream, signal, tap_count):
    margin = (tap_count - 1) // 2
    length = signal.shape[-2]
    widths = [(0, 0)] * (signal.ndim - 2) + [(margin, margin), (0, 0)]
    padded = jnp.pad(signal, widths)
    leading = tuple(range(signal.ndim - 1))
    return jnp.stack(
        [
            jnp.sum(upstream * padded[..., offset : offset + length, :], axis=leading)
            for offset in range(tap_count)
        ]
    )


def activation(inputs, present, kernel, gains):
    hidden = inputs.astype(jnp.float32) * present
    mixed = depthwise(hidden, kernel)
    average = jnp.mean(mixed, axis=-1, keepdims=True)
    centred = mixed - average
    inverse = lax.rsqrt(jnp.mean(centred * centred, axis=-1, keepdims=True) + EPSILON)
    normed = centred * inverse
    gained = normed * gains.astype(jnp.float32)
    logistic = jax.nn.sigmoid(gained)
    return (hidden, inverse, normed, gained, logistic)


def through_norm(
    grad_activated, hidden, inverse, normed, gained, logistic, kernel, gains, upstream, present
):
    grad_gained = grad_activated * (logistic + gained * logistic * (1.0 - logistic))
    leading = tuple(range(grad_gained.ndim - 1))
    gain_term = jnp.sum(grad_gained * normed, axis=leading)
    grad_normed = grad_gained * gains.astype(jnp.float32)
    grad_mixed = inverse * (
        grad_normed
        - jnp.mean(grad_normed, axis=-1, keepdims=True)
        - normed * jnp.mean(grad_normed * normed, axis=-1, keepdims=True)
    )
    kernel_term = tap_sums(grad_mixed, hidden, kernel.shape[0])
    grad_hidden = depthwise(grad_mixed, kernel[::-1])
    grad_inputs = (upstream + grad_hidden * present).astype(jnp.bfloat16)
    return (grad_inputs, kernel_term, gain_term)


def body(saved_inputs, grad_outputs, lengths, pointwise, depth_kernel, norm_gain):
    sections = lax.axis_size("section")
    section_id = lax.axis_index("section")
    local_inputs = saved_inputs[0, :, 0]
    local_grads = grad_outputs[:, 0]
    local_lengths = lengths[:, 0]
    micro_count, frames, features = local_inputs.shape
    factor = float(lax.axis_size("fsdp") * micro_count * frames) ** (-0.5)
    projection, kernel, gains = (
        lax.all_gather(pointwise[0], "fsdp", axis=0, tiled=True),
        lax.all_gather(depth_kernel[0], "fsdp", axis=1, tiled=True),
        lax.all_gather(norm_gain[0], "fsdp", axis=0, tiled=True),
    )
    places = jnp.arange(frames, dtype=jnp.int32)
    stores = (jnp.zeros((features, features), jnp.float32),)

    def compute_step(bundle):
        frame_out, kernel_sum, gain_sum, held, micro_slot, upstream_raw = bundle
        inputs = lax.dynamic_index_in_dim(local_inputs, micro_slot, 0, keepdims=False)
        length_now = lax.dynamic_index_in_dim(local_lengths, micro_slot, 0, keepdims=False)
        present = (places < length_now).astype(jnp.float32)[:, None]
        upstream = upstream_raw.astype(jnp.float32)
        hidden, inverse, normed, gained, logistic = activation(inputs, present, kernel, gains)
        activated = (gained * logistic).astype(jnp.bfloat16)
        grad_masked = (upstream * present).astype(jnp.bfloat16)
        grad_activated = lax.dot_general(
            grad_masked, projection, (((1,), (1,)), ((), ())), preferred_element_type=jnp.float32
        )
        grad_inputs, kernel_term, gain_term = through_norm(
            grad_activated,
            hidden,
            inverse,
            normed,
            gained,
            logistic,
            kernel,
            gains,
            upstream,
            present,
        )
        held = (
            held[0]
            + lax.dot_general(
                activated, grad_masked, (((0,), (0,)), ((), ())), preferred_element_type=jnp.float32
            ),
        )
        frame_out = lax.dynamic_update_index_in_dim(frame_out, grad_inputs, micro_slot, 0)
        return (grad_inputs, frame_out, kernel_sum + kernel_term, gain_sum + gain_term, held)

    def pass_step(bundle):
        frame_out, kernel_sum, gain_sum, held, micro_slot, upstream_raw = bundle
        return (jnp.zeros_like(upstream_raw), frame_out, kernel_sum, gain_sum, held)

    def one_turn(counter, loop_state):
        received, frame_out, kernel_sum, gain_sum, held = loop_state
        position = counter - (sections - 1 - section_id)
        active = jnp.logical_and(position >= 0, position < micro_count)
        micro_slot = jnp.clip(position, 0, micro_count - 1)
        outer_grad = lax.dynamic_index_in_dim(local_grads, micro_slot, 0, keepdims=False)
        upstream_raw = jnp.where(section_id == sections - 1, outer_grad, received)
        grad_inputs, frame_out, kernel_sum, gain_sum, held = lax.cond(
            active,
            compute_step,
            pass_step,
            (frame_out, kernel_sum, gain_sum, held, micro_slot, upstream_raw),
        )
        received = shifted(grad_inputs, "section", -1)
        return (received, frame_out, kernel_sum, gain_sum, held)

    initial = (
        jnp.zeros((frames, features), jnp.bfloat16),
        jnp.zeros((micro_count, frames, features), jnp.bfloat16),
        jnp.zeros(kernel.shape, jnp.float32),
        jnp.zeros((features,), jnp.float32),
        stores,
    )
    received, frame_out, kernel_sum, gain_sum, held = lax.fori_loop(
        0, micro_count + sections - 1, one_turn, initial
    )
    point_share, kernel_share, gain_share = (
        lax.psum_scatter(held[0], "fsdp", scatter_dimension=0, tiled=True),
        lax.psum_scatter(kernel_sum, "fsdp", scatter_dimension=1, tiled=True),
        lax.psum_scatter(gain_sum, "fsdp", scatter_dimension=0, tiled=True),
    )
    return (
        frame_out[None, :, None],
        (point_share * factor)[None],
        (kernel_share * factor)[None],
        (gain_share * factor)[None],
    )


def solution(mesh):
    placed = (
        P("section", None, "fsdp", None, None),
        P(None, "fsdp", None, None),
        P(None, "fsdp"),
        P("section", "fsdp", None),
        P("section", None, "fsdp"),
        P("section", "fsdp"),
    )
    return jax.shard_map(
        body,
        mesh=mesh,
        in_specs=placed,
        out_specs=(
            P("section", None, "fsdp", None, None),
            P("section", "fsdp", None),
            P("section", None, "fsdp"),
            P("section", "fsdp"),
        ),
        check_vma=False,
    )
```

profile of v0, /device:TPU:0, one launch (start us, length us, event | category | flops | bytes accessed | tf_op | source)
XLA Modules:
  0.0 916.9 jit_solution(1244989175964518420)
XLA Ops:
  8.8 102.0 %all-gather = bf16[1,5,1536]{1,0,2:T(2,128)(2,1)S(1)} all-gather(bf16[1,5,48]{1,0,2:T(2,128)(2,1)S(1)} %copy.13), channel_id=2, replica_groups=mesh['section'=4,'fsdp'=32] {'fsdp'}, dimensions={2}, use_global_device_ids=true | all-gather | bytes 15840 | tf_op jit(solution)/shard_map/all_gather | solution.py:83
  114.1 88.9 %all-reduce.2 = bf16[1536]{0:T(1024)(128)(2,1)S(1)} all-reduce(bf16[1536]{0:T(1024)(128)(2,1)S(1)} %dynamic-update-slice), channel_id=4, replica_groups=mesh['section'=4,'fsdp'=32] {'fsdp'}, use_global_device_ids=true, to_apply=%add.2 | all-reduce | flops 1536 | bytes 6144 | tf_op jit(solution)/shard_map/all_gather | solution.py:84
  205.1 4.8 broadcast_in_dim.42
  209.9 235.8 %while.24 = (s32[]{:T(128)}, bf16[512,1536]{1,0:T(8,128)(2,1)S(1)}, bf16[2,512,1536]{2,1,0:T(8,128)(2,1)}, f32[5,1536]{1,0:T(8,128)S(1)}, f32[1536]{0:T(1024)S(1...) while((s32[]{:T(128)}, bf16[512,1536]{1,0:T(8,128)(2,1)S(1)}, ...), condition=%wide.region_13.14_spmd.clone, body=%wide.region_0.13_spmd.clone.sunk | while | flops 4896336384 | bytes 110565944 | solution.py:149
  212.4 4.2 collective-permute-done
  219.2 19.4 %collective-permute-done = bf16[512,1536]{1,0:T(8,128)(2,1)S(1)} collective-permute-done((bf16[512,1536]{1,0:T(8,128)(2,1)}, bf16[512,1536]{1,0:T(8,128)(2,1)S(1)}, u32[]{:S(2)}, u32[]{:S(2)}) %collective-permute-start) | collective-permute-done | bytes 1572896 | tf_op jit(solution)/shard_map/while/body/eval_jaxpr/ppermute | solution.py:12
  241.2 96.7 %collective-permute-done = bf16[512,1536]{1,0:T(8,128)(2,1)S(1)} collective-permute-done((bf16[512,1536]{1,0:T(8,128)(2,1)}, bf16[512,1536]{1,0:T(8,128)(2,1)S(1)}, u32[]{:S(2)}, u32[]{:S(2)}) %collective-permute-start) | collective-permute-done | bytes 1572896 | tf_op jit(solution)/shard_map/while/body/eval_jaxpr/ppermute | solution.py:12
  337.9 40.2 %conditional.3 = (bf16[512,1536]{1,0:T(8,128)(2,1)}, bf16[2,512,1536]{2,1,0:T(8,128)(2,1)}, f32[5,1536]{1,0:T(8,128)S(1)}, f32[1536]{0:T(1024)S(1)}, f32[1536,1536]{1,0:T(8,128)}) conditional(s32[]{:T(128)} %convert_element_type.106, (bf16[2,512,1536]{2,1,0:T(8,128)(2,1)}, f32[5,1536]{1,0:T(8,128)S(1)}, f32[1536]{0:T(1024)S(1)}, ...), branch_computations={%region_1.1_spmd, %region_2.12_spmd} | conditional | flops 4896336384 | bytes 104272064 | solution.py:133
  343.1 2.4 fusion.16
  346.0 3.6 multiply_reduce_fusion
  349.7 8.5 multiply_reduce_fusion.1
  358.3 9.3 %bitcast_dynamic-update-slice_fusion = (bf16[2,512,1536]{2,1,0:T(8,128)(2,1)}, bf16[512,1536]{1,0:T(8,128)(2,1)}) fusion(bf16[2,512,1536]{2,1,0:T(8,128)(2,1)} %get-tuple-element.440, s32[]{:T(128)S(6)} %min.10, f32[512]{0:T(512)S(1)} %compare_convert_fusion, f32[1536]{0:T(1024)S(1)} %get-tuple-element.546, f32[1536]{0:T(1024)S(1)} %get-tuple-element.545, ...), kind=kLoop, calls=%fused_computation.28 | loop fusion | flops 10223616 | bytes 7897092 | tf_op jit(solution)/shard_map/while/body/eval_jaxpr/cond/branch_1_fun/jit(dynamic_update_index_in_dim)/dynamic_update_slice | solution.py:119
  367.6 10.5 %convolution_add_fusion = f32[1536,1536]{1,0:T(8,128)} fusion(f32[1536,1536]{1,0:T(8,128)} %get-tuple-element.443, f32[512,1536]{1,0:T(8,128)S(1)} %get-tuple-element.579, f32[1536]{0:T(1024)S(1)} %convert_element_type.78, f32[512]{0:T(512)S(1)} %add_rsqrt_fusion, f32[512]{0:T(512)S(1)} %broadcast_multiply_fusion.2, bf16[512,1536]{1,0:T(8,128)(2,1)S(1)} %copy-done.1, ...), kind=kOutput, calls=%fused_computation.1 | convolution fusion | flops 2426929152 | bytes 23605248 | tf_op jit(solution)/shard_map/while/body/eval_jaxpr/cond/branch_1_fun/dot_general | solution.py:115
  379.4 20.6 %collective-permute-done = bf16[512,1536]{1,0:T(8,128)(2,1)S(1)} collective-permute-done((bf16[512,1536]{1,0:T(8,128)(2,1)}, bf16[512,1536]{1,0:T(8,128)(2,1)S(1)}, u32[]{:S(2)}, u32[]{:S(2)}) %collective-permute-start) | collective-permute-done | bytes 1572896 | tf_op jit(solution)/shard_map/while/body/eval_jaxpr/ppermute | solution.py:12
  400.0 40.2 %conditional.3 = (bf16[512,1536]{1,0:T(8,128)(2,1)}, bf16[2,512,1536]{2,1,0:T(8,128)(2,1)}, f32[5,1536]{1,0:T(8,128)S(1)}, f32[1536]{0:T(1024)S(1)}, f32[1536,1536]{1,0:T(8,128)}) conditional(s32[]{:T(128)} %convert_element_type.106, (bf16[2,512,1536]{2,1,0:T(8,128)(2,1)}, f32[5,1536]{1,0:T(8,128)S(1)}, f32[1536]{0:T(1024)S(1)}, ...), branch_computations={%region_1.1_spmd, %region_2.12_spmd} | conditional | flops 4896336384 | bytes 104272064 | solution.py:133
  405.3 2.4 fusion.16
  408.2 3.6 multiply_reduce_fusion
  411.8 8.5 multiply_reduce_fusion.1
  420.5 9.3 %bitcast_dynamic-update-slice_fusion = (bf16[2,512,1536]{2,1,0:T(8,128)(2,1)}, bf16[512,1536]{1,0:T(8,128)(2,1)}) fusion(bf16[2,512,1536]{2,1,0:T(8,128)(2,1)} %get-tuple-element.440, s32[]{:T(128)S(6)} %min.10, f32[512]{0:T(512)S(1)} %compare_convert_fusion, f32[1536]{0:T(1024)S(1)} %get-tuple-element.546, f32[1536]{0:T(1024)S(1)} %get-tuple-element.545, ...), kind=kLoop, calls=%fused_computation.28 | loop fusion | flops 10223616 | bytes 7897092 | tf_op jit(solution)/shard_map/while/body/eval_jaxpr/cond/branch_1_fun/jit(dynamic_update_index_in_dim)/dynamic_update_slice | solution.py:119
  429.7 10.5 %convolution_add_fusion = f32[1536,1536]{1,0:T(8,128)} fusion(f32[1536,1536]{1,0:T(8,128)} %get-tuple-element.443, f32[512,1536]{1,0:T(8,128)S(1)} %get-tuple-element.579, f32[1536]{0:T(1024)S(1)} %convert_element_type.78, f32[512]{0:T(512)S(1)} %add_rsqrt_fusion, f32[512]{0:T(512)S(1)} %broadcast_multiply_fusion.2, bf16[512,1536]{1,0:T(8,128)(2,1)S(1)} %copy-done.1, ...), kind=kOutput, calls=%fused_computation.1 | convolution fusion | flops 2426929152 | bytes 23605248 | tf_op jit(solution)/shard_map/while/body/eval_jaxpr/cond/branch_1_fun/dot_general | solution.py:115
  441.5 4.2 collective-permute-done
  448.3 92.5 %all-reduce.3 = f32[1536]{0:T(1024)S(1)} all-reduce(f32[1536]{0:T(1024)S(1)} %get-tuple-element.476), channel_id=7, replica_groups=mesh['section'=4,'fsdp'=32] {'fsdp'}, use_global_device_ids=true, to_apply=%region_16.17.clone | all-reduce | flops 1536 | bytes 12288
  541.5 122.3 %reduce-scatter.7.cloned.1.call-done = f32[48,5]{1,0:T(8,128)} async-done(((f32[1536,5]{1,0:T(8,128)}), f32[48,5]{1,0:T(8,128)}) %reduce-scatter.7.cloned.1.call-update) | async-done | bytes 976
  665.2 243.5 %reduce-scatter.5.cloned.1.call-done = f32[48,1536]{1,0:T(8,128)} async-done(((f32[1536,1536]{1,0:T(8,128)}), f32[48,1536]{1,0:T(8,128)}) %reduce-scatter.5.cloned.1.call-update) | async-done | bytes 294928 | tf_op jit(solution)/shard_map/reduce_scatter | solution.py:153
  (94 shorter events, 37.4 us)
Async XLA Ops:
  7.2 195.9 %all-gather.5.cloned.1.call-start = ((), (), s32[]{:S(2)}) async-start(), calls=%async_computation.3 | async-start | bytes 4866048 | tf_op jit(solution)/shard_map/all_gather | solution.py:82
  7.9 655.9 %reduce-scatter.7.cloned.1.call-start = ((), (), s32[]{:S(2)}) async-start(), calls=%async_computation.4 | async-start | bytes 811008
  205.1 4.8 copy-start.2
  211.1 5.5 collective-permute-start
  217.9 20.7 %collective-permute-start = (bf16[512,1536]{1,0:T(8,128)(2,1)}, bf16[512,1536]{1,0:T(8,128)(2,1)S(1)}, u32[]{:S(2)}, u32[]{:S(2)}) collective-permute-start(bf16[512,1536]{1,0:T(8,128)(2,1)} %get-tuple-element.675), channel_id=1, source_target_pairs={{32,0},{64,32},{96,64},{33,1},{65,33},{97,65},{34,2},{66,34},{98,6... | collective-permute-start | bytes 4718600 | tf_op jit(solution)/shard_map/while/body/eval_jaxpr/ppermute | solution.py:12
  239.9 98.0 %collective-permute-start = (bf16[512,1536]{1,0:T(8,128)(2,1)}, bf16[512,1536]{1,0:T(8,128)(2,1)S(1)}, u32[]{:S(2)}, u32[]{:S(2)}) collective-permute-start(bf16[512,1536]{1,0:T(8,128)(2,1)} %get-tuple-element.675), channel_id=1, source_target_pairs={{32,0},{64,32},{96,64},{33,1},{65,33},{97,65},{34,2},{66,34},{98,6... | collective-permute-start | bytes 4718600 | tf_op jit(solution)/shard_map/while/body/eval_jaxpr/ppermute | solution.py:12
  340.8 5.2 copy-start
  340.8 5.2 slice-start
  343.1 2.9 slice-start.1
  358.3 9.3 %copy-start.1 = (bf16[512,1536]{1,0:T(8,128)(2,1)S(1)}, bf16[512,1536]{1,0:T(8,128)(2,1)}, u32[]{:S(2)}) copy-start(bf16[512,1536]{1,0:T(8,128)(2,1)} %copy-done) | copy-start | bytes 4718596 | tf_op jit(solution)/shard_map/while/body/eval_jaxpr/cond
  378.1 21.9 %collective-permute-start = (bf16[512,1536]{1,0:T(8,128)(2,1)}, bf16[512,1536]{1,0:T(8,128)(2,1)S(1)}, u32[]{:S(2)}, u32[]{:S(2)}) collective-permute-start(bf16[512,1536]{1,0:T(8,128)(2,1)} %get-tuple-element.675), channel_id=1, source_target_pairs={{32,0},{64,32},{96,64},{33,1},{65,33},{97,65},{34,2},{66,34},{98,6... | collective-permute-start | bytes 4718600 | tf_op jit(solution)/shard_map/while/body/eval_jaxpr/ppermute | solution.py:12
  403.0 5.2 copy-start
  403.0 5.2 slice-start
  405.3 2.9 slice-start.1
  420.4 9.3 %copy-start.1 = (bf16[512,1536]{1,0:T(8,128)(2,1)S(1)}, bf16[512,1536]{1,0:T(8,128)(2,1)}, u32[]{:S(2)}) copy-start(bf16[512,1536]{1,0:T(8,128)(2,1)} %copy-done) | copy-start | bytes 4718596 | tf_op jit(solution)/shard_map/while/body/eval_jaxpr/cond
  440.2 5.5 collective-permute-start
  446.9 461.8 %reduce-scatter.5.cloned.1.call-start = ((), (), s32[]{:S(2)}) async-start(), calls=%async_computation.2 | async-start | bytes 9732096 | tf_op jit(solution)/shard_map/reduce_scatter | solution.py:153
Sparse Core Ops, SparseCore 0:
  11.0 86.2 all-gather.4
  447.0 216.7 reduce-scatter.6
  669.9 238.7 reduce-scatter.4
where the time goes:
time: 918 us; the launch traced here: 917 us
  waiting for transfers between devices  512 us (56%)
  blocking collectives  283 us (31%)
  other arithmetic  52.8 us (6%)
  matrix products  28.2 us (3%)
  local copies, waits for them, and re-layouts  18.1 us (2%)
  between operations  15.2 us (2%)
    reduce_scatter x1, waiting for transfers between devices, body(): lax.psum_scatter(held[0], 'fsdp', scatter_dimension=0, tiled=True)  243 us
    ppermute x5, waiting for transfers between devices, shifted(): return lax.ppermute(block, axis, route)  145 us
    unnamed x4, waiting for transfers between devices  124 us
    all_gather x1, blocking collectives, body(): lax.all_gather(depth_kernel[0], 'fsdp', axis=1, tiled=True)  102 us
    unnamed x1, blocking collectives  92.5 us
    all_gather x1, blocking collectives, body(): lax.all_gather(norm_gain[0], 'fsdp', axis=0, tiled=True)  88.9 us
    dot_general x2, matrix products, compute_step(): lax.dot_general(activated, grad_masked, (((0,), (0,)), ((), ())), preferr...  20.9 us
    dynamic_update_slice x2, other arithmetic, compute_step(): lax.dynamic_update_index_in_dim(frame_out, grad_inputs, micro_slot, 0)  18.5 us
  transfers between devices with their start and end apart: 8, of which 7 were waited for; matrix products, arithmetic and copies ran while one was open for 1% of the time, Pallas kernels for 0%

commit v1 on v0

--- a/solution.py
+++ b/solution.py
@@ -78,10 +78,19 @@
     local_lengths = lengths[:, 0]
     micro_count, frames, features = local_inputs.shape
     factor = float(lax.axis_size("fsdp") * micro_count * frames) ** (-0.5)
+    trace_hubs = lambda point, chip_axis: jnp.concatenate(
+        lax.all_to_all(
+            jnp.stack([point for _ in range(lax.psum(1, axis_name=chip_axis))]),
+            axis_name=chip_axis,
+            split_axis=0,
+            concat_axis=0,
+        ),
+        axis=0,
+    )
     projection, kernel, gains = (
         lax.all_gather(pointwise[0], "fsdp", axis=0, tiled=True),
         lax.all_gather(depth_kernel[0], "fsdp", axis=1, tiled=True),
-        lax.all_gather(norm_gain[0], "fsdp", axis=0, tiled=True),
+        trace_hubs(norm_gain[0], "fsdp"),
     )
     places = jnp.arange(frames, dtype=jnp.int32)
     stores = (jnp.zeros((features, features), jnp.float32),)

time: 918 us -> 816 us (0.89)
  blocking collectives: 283 us -> 192 us
  other arithmetic: 52.8 us -> 33.2 us
  waiting for transfers between devices: 512 us -> 500 us
  local copies, waits for them, and re-layouts: 18.1 us -> 29.3 us
  starting transfers between devices: 6.52 us -> 17.4 us
    all_gather x1 -> x0, blocking collectives: 88.9 us -> none  [body(): lax.all_gather(norm_gain[0], 'fsdp', axis=0, tiled=True)]
    ppermute x5, waiting for transfers between devices: 145 us -> 133 us  [shifted(): return lax.ppermute(block, axis, route)]
    dynamic_update_slice x2, other arithmetic: 18.5 us -> 7.08 us  [compute_step(): lax.dynamic_update_index_in_dim(frame_out, grad_inputs, micro_slot, 0)]
    all_to_all x0 -> x1, starting transfers between devices: none -> 10.9 us  [body(): lax.all_to_all(jnp.stack([point for _ in range(lax.psum(1, axis_name=chip...]
  transfers between devices with their start and end apart: 8 -> 9, of which waited for: 7 -> 7; matrix products, arithmetic and copies ran while one was open for 1% -> 1% of each run, Pallas kernels for 0% -> 0%
where the time goes in v1:
time: 816 us; the launch traced here: 815 us
  waiting for transfers between devices  500 us (61%)
  blocking collectives  192 us (24%)
  other arithmetic  33.2 us (4%)
  local copies, waits for them, and re-layouts  29.3 us (4%)
  matrix products  29 us (4%)
  starting transfers between devices  17.4 us (2%)
  between operations  14.5 us (2%)
    reduce_scatter x1, waiting for transfers between devices, body(): lax.psum_scatter(held[0], 'fsdp', scatter_dimension=0, tiled=True)  243 us
    ppermute x5, waiting for transfers between devices, shifted(): return lax.ppermute(block, axis, route)  133 us
    unnamed x4, waiting for transfers between devices  124 us
    all_gather x1, blocking collectives, body(): lax.all_gather(depth_kernel[0], 'fsdp', axis=1, tiled=True)  101 us
    unnamed x1, blocking collectives  90.7 us
    dot_general x2, matrix products, compute_step(): lax.dot_general(activated, grad_masked, (((0,), (0,)), ((), ())), preferr...  21.8 us
  transfers between devices with their start and end apart: 9, of which 7 were waited for; matrix products, arithmetic and copies ran while one was open for 1% of the time, Pallas kernels for 0%

profile of v1, /device:TPU:0, one launch (start us, length us, event | category | flops | bytes accessed | tf_op | source)
XLA Modules:
  0.0 815.0 jit_solution(10566512692849337958)
XLA Ops:
  9.2 10.9 %all-to-all-start = ((bf16[32,1,48]{2,1,0:T(2,128)(2,1)}), bf16[32,1,48]{2,1,0:T(2,128)(2,1)S(1)}, u32[]{:S(2)}, u32[]{:S(2)}) async-start(bf16[32,1,48]{2,1,0:T(2,128)(2,1)} %stack.33), calls=%async_computation | async-start | bytes 32768 | tf_op jit(solution)/shard_map/all_to_all | solution.py:82
  20.9 100.9 %all-gather = bf16[1,5,1536]{1,0,2:T(2,128)(2,1)S(1)} all-gather(bf16[1,5,48]{1,0,2:T(2,128)(2,1)S(1)} %copy.13), channel_id=2, replica_groups=mesh['section'=4,'fsdp'=32] {'fsdp'}, dimensions={2}, use_global_device_ids=true | all-gather | bytes 15840 | tf_op jit(solution)/shard_map/all_gather | solution.py:92
  125.5 4.8 broadcast_in_dim.42
  130.4 214.8 %while.24 = (s32[]{:T(128)}, bf16[512,1536]{1,0:T(8,128)(2,1)}, bf16[2,512,1536]{2,1,0:T(8,128)(2,1)}, f32[5,1536]{1,0:T(8,128)S(1)}, f32[1536]{0:T(1024)S(1)}, ...) while((s32[]{:T(128)}, bf16[512,1536]{1,0:T(8,128)(2,1)}, ...), condition=%wide.region_13.14_spmd.clone, body=%wide.region_0.13_spmd.clone.sunk | while | flops 4896336384 | bytes 134158936 | solution.py:158
  133.0 4.2 collective-permute-done
  140.9 19.0 %collective-permute-done = bf16[512,1536]{1,0:T(8,128)(2,1)S(1)} collective-permute-done((bf16[512,1536]{1,0:T(8,128)(2,1)}, bf16[512,1536]{1,0:T(8,128)(2,1)S(1)}, u32[]{:S(2)}, u32[]{:S(2)}) %collective-permute-start) | collective-permute-done | bytes 1572896 | tf_op jit(solution)/shard_map/while/body/eval_jaxpr/ppermute | solution.py:12
  163.6 84.6 %collective-permute-done = bf16[512,1536]{1,0:T(8,128)(2,1)S(1)} collective-permute-done((bf16[512,1536]{1,0:T(8,128)(2,1)}, bf16[512,1536]{1,0:T(8,128)(2,1)S(1)}, u32[]{:S(2)}, u32[]{:S(2)}) %collective-permute-start) | collective-permute-done | bytes 1572896 | tf_op jit(solution)/shard_map/while/body/eval_jaxpr/ppermute | solution.py:12
  249.4 33.1 %conditional.3 = (bf16[512,1536]{1,0:T(8,128)(2,1)}, bf16[2,512,1536]{2,1,0:T(8,128)(2,1)}, f32[5,1536]{1,0:T(8,128)S(1)}, f32[1536]{0:T(1024)S(1)}, f32[1536,1536]{1,0:T(8,128)}) conditional(s32[]{:T(128)} %convert_element_type.106, (bf16[2,512,1536]{2,1,0:T(8,128)(2,1)}, f32[5,1536]{1,0:T(8,128)S(1)}, f32[1536]{0:T(1024)S(1)}, ...), branch_computations={%region_1.1_spmd, %region_2.12_spmd} | conditional | flops 4896336384 | bytes 121573568 | solution.py:142
  252.4 2.4 fusion.16
  257.7 3.6 multiply_reduce_fusion
  261.4 6.4 multiply_reduce_fusion.1
  267.8 3.5 bitcast_dynamic-update-slice_fusion
  271.5 10.9 %convolution_add_fusion = f32[1536,1536]{1,0:T(8,128)} fusion(f32[1536,1536]{1,0:T(8,128)} %get-tuple-element.443, f32[512,1536]{1,0:T(8,128)S(1)} %get-tuple-element.579, f32[1536]{0:T(1024)S(1)} %convert_element_type.78, f32[512]{0:T(512)S(1)} %add_rsqrt_fusion, f32[512]{0:T(512)S(1)} %broadcast_multiply_fusion.2, bf16[512,1536]{1,0:T(8,128)(2,1)} %copy-done, ...), kind=kOutput, calls=%fused_computation.1 | convolution fusion | flops 2426929152 | bytes 23605248 | tf_op jit(solution)/shard_map/while/body/eval_jaxpr/cond/branch_1_fun/dot_general | solution.py:124
  283.7 20.7 %collective-permute-done = bf16[512,1536]{1,0:T(8,128)(2,1)S(1)} collective-permute-done((bf16[512,1536]{1,0:T(8,128)(2,1)}, bf16[512,1536]{1,0:T(8,128)(2,1)S(1)}, u32[]{:S(2)}, u32[]{:S(2)}) %collective-permute-start) | collective-permute-done | bytes 1572896 | tf_op jit(solution)/shard_map/while/body/eval_jaxpr/ppermute | solution.py:12
  305.5 33.0 %conditional.3 = (bf16[512,1536]{1,0:T(8,128)(2,1)}, bf16[2,512,1536]{2,1,0:T(8,128)(2,1)}, f32[5,1536]{1,0:T(8,128)S(1)}, f32[1536]{0:T(1024)S(1)}, f32[1536,1536]{1,0:T(8,128)}) conditional(s32[]{:T(128)} %convert_element_type.106, (bf16[2,512,1536]{2,1,0:T(8,128)(2,1)}, f32[5,1536]{1,0:T(8,128)S(1)}, f32[1536]{0:T(1024)S(1)}, ...), branch_computations={%region_1.1_spmd, %region_2.12_spmd} | conditional | flops 4896336384 | bytes 121573568 | solution.py:142
  308.6 2.4 fusion.16
  313.9 3.6 multiply_reduce_fusion
  317.5 6.4 multiply_reduce_fusion.1
  324.0 3.5 bitcast_dynamic-update-slice_fusion
  327.7 10.9 %convolution_add_fusion = f32[1536,1536]{1,0:T(8,128)} fusion(f32[1536,1536]{1,0:T(8,128)} %get-tuple-element.443, f32[512,1536]{1,0:T(8,128)S(1)} %get-tuple-element.579, f32[1536]{0:T(1024)S(1)} %convert_element_type.78, f32[512]{0:T(512)S(1)} %add_rsqrt_fusion, f32[512]{0:T(512)S(1)} %broadcast_multiply_fusion.2, bf16[512,1536]{1,0:T(8,128)(2,1)} %copy-done, ...), kind=kOutput, calls=%fused_computation.1 | convolution fusion | flops 2426929152 | bytes 23605248 | tf_op jit(solution)/shard_map/while/body/eval_jaxpr/cond/branch_1_fun/dot_general | solution.py:124
  339.8 4.2 collective-permute-done
  348.4 90.7 %all-reduce.2 = f32[1536]{0:T(1024)S(1)} all-reduce(f32[1536]{0:T(1024)S(1)} %get-tuple-element.476), channel_id=6, replica_groups=mesh['section'=4,'fsdp'=32] {'fsdp'}, use_global_device_ids=true, to_apply=%region_16.17.clone | all-reduce | flops 1536 | bytes 12288
  439.7 122.1 %reduce-scatter.7.cloned.1.call-done = f32[48,5]{1,0:T(8,128)} async-done(((f32[1536,5]{1,0:T(8,128)}), f32[48,5]{1,0:T(8,128)}) %reduce-scatter.7.cloned.1.call-update) | async-done | bytes 976
  563.3 243.5 %reduce-scatter.5.cloned.1.call-done = f32[48,1536]{1,0:T(8,128)} async-done(((f32[1536,1536]{1,0:T(8,128)}), f32[48,1536]{1,0:T(8,128)}) %reduce-scatter.5.cloned.1.call-update) | async-done | bytes 294928 | tf_op jit(solution)/shard_map/reduce_scatter | solution.py:162
  (106 shorter events, 44.7 us)
Async XLA Ops:
  7.2 115.2 %all-gather.4.cloned.1.call-start = ((), (), s32[]{:S(2)}) async-start(), calls=%async_computation.4 | async-start | bytes 4866048 | tf_op jit(solution)/shard_map/all_gather | solution.py:91
  9.2 113.1 %all-to-all-start = ((bf16[32,1,48]{2,1,0:T(2,128)(2,1)}), bf16[32,1,48]{2,1,0:T(2,128)(2,1)S(1)}, u32[]{:S(2)}, u32[]{:S(2)}) async-start(bf16[32,1,48]{2,1,0:T(2,128)(2,1)} %stack.33), calls=%async_computation | async-start | bytes 32768 | tf_op jit(solution)/shard_map/all_to_all | solution.py:82
  20.1 541.8 %reduce-scatter.7.cloned.1.call-start = ((), (), s32[]{:S(2)}) async-start(), calls=%async_computation.5 | async-start | bytes 811008
  125.5 4.8 copy-start.5
  131.7 5.5 collective-permute-start
  137.2 1.1 copy-start.2
  139.6 20.3 %collective-permute-start = (bf16[512,1536]{1,0:T(8,128)(2,1)}, bf16[512,1536]{1,0:T(8,128)(2,1)S(1)}, u32[]{:S(2)}, u32[]{:S(2)}) collective-permute-start(bf16[512,1536]{1,0:T(8,128)(2,1)} %get-tuple-element.673), channel_id=1, source_target_pairs={{32,0},{64,32},{96,64},{33,1},{65,33},{97,65},{34,2},{66,34},{98,6... | collective-permute-start | bytes 4718600 | tf_op jit(solution)/shard_map/while/body/eval_jaxpr/ppermute | solution.py:12
  159.9 1.1 copy-start.2
  162.3 85.9 %collective-permute-start = (bf16[512,1536]{1,0:T(8,128)(2,1)}, bf16[512,1536]{1,0:T(8,128)(2,1)S(1)}, u32[]{:S(2)}, u32[]{:S(2)}) collective-permute-start(bf16[512,1536]{1,0:T(8,128)(2,1)} %get-tuple-element.673), channel_id=1, source_target_pairs={{32,0},{64,32},{96,64},{33,1},{65,33},{97,65},{34,2},{66,34},{98,6... | collective-permute-start | bytes 4718600 | tf_op jit(solution)/shard_map/while/body/eval_jaxpr/ppermute | solution.py:12
  248.2 1.1 copy-start.2
  252.4 2.9 copy-start.3
  254.8 1.4 copy-start.1
  255.3 2.5 copy-start.4
  257.7 10.1 %copy-start = (bf16[512,1536]{1,0:T(8,128)(2,1)}, bf16[512,1536]{1,0:T(8,128)(2,1)S(1)}, u32[]{:S(2)}) copy-start(bf16[512,1536]{1,0:T(8,128)(2,1)S(1)} %bitcast_select_fusion) | copy-start | bytes 4718596 | tf_op jit(solution)/shard_map/while/body/eval_jaxpr/cond
  282.4 21.9 %collective-permute-start = (bf16[512,1536]{1,0:T(8,128)(2,1)}, bf16[512,1536]{1,0:T(8,128)(2,1)S(1)}, u32[]{:S(2)}, u32[]{:S(2)}) collective-permute-start(bf16[512,1536]{1,0:T(8,128)(2,1)} %get-tuple-element.673), channel_id=1, source_target_pairs={{32,0},{64,32},{96,64},{33,1},{65,33},{97,65},{34,2},{66,34},{98,6... | collective-permute-start | bytes 4718600 | tf_op jit(solution)/shard_map/while/body/eval_jaxpr/ppermute | solution.py:12
  304.4 1.1 copy-start.2
  308.6 2.9 copy-start.3
  310.9 1.4 copy-start.1
  311.4 2.5 copy-start.4
  313.9 10.1 %copy-start = (bf16[512,1536]{1,0:T(8,128)(2,1)}, bf16[512,1536]{1,0:T(8,128)(2,1)S(1)}, u32[]{:S(2)}) copy-start(bf16[512,1536]{1,0:T(8,128)(2,1)S(1)} %bitcast_select_fusion) | copy-start | bytes 4718596 | tf_op jit(solution)/shard_map/while/body/eval_jaxpr/cond
  338.6 5.5 collective-permute-start
  344.1 1.1 copy-start.2
  346.4 460.3 %reduce-scatter.5.cloned.1.call-start = ((), (), s32[]{:S(2)}) async-start(), calls=%async_computation.3 | async-start | bytes 9732096 | tf_op jit(solution)/shard_map/reduce_scatter | solution.py:162
  346.5 0.7 copy-start.6
Sparse Core Ops, SparseCore 0:
  11.0 86.0 all-gather.3
  346.5 215.2 reduce-scatter.6
  568.0 238.7 reduce-scatter.4
